TPU v7x, 32 devices: a whole 2x2x4 slice. The times are simulated.
32 devices in a mesh: grp: 1, row: 32 (over z, y, x, core).
Axes of the slice: x: 2, y: 2, z: 4, core: 2. Of those that a mesh axis runs over, the one named last changes fastest.
Arguments:
- pair_map: bfloat16 [128, 128, 128], P(('grp', 'row')), may hold values from -6 to 6
- single: bfloat16 [128, 384], P(('grp', 'row')), may hold values from -6 to 6
- noise_term: bfloat16 [128, 384], P(('grp', 'row')), may hold values from -3 to 3
- token_mask: int32 [128], P('grp'), may hold values 0 or 1
- w_mul_in: bfloat16 [128, 512], replicated, may hold values from -0.5 to 0.5
- w_mul_gate: bfloat16 [128, 128], replicated, may hold values from -0.5 to 0.5
- w_mul_out: bfloat16 [128, 128], replicated, may hold values from -0.5 to 0.5
- w_att_in: bfloat16 [128, 512], replicated, may hold values from -0.5 to 0.5
- w_att_bias: bfloat16 [128, 4], replicated, may hold values from -0.5 to 0.5
- w_att_out: bfloat16 [128, 128], replicated, may hold values from -0.5 to 0.5
- w_tok_in: bfloat16 [384, 1536], replicated, may hold values from -0.3125 to 0.3125
- w_pair_bias: bfloat16 [128, 16], replicated, may hold values from -0.5 to 0.5
- w_tok_out: bfloat16 [384, 384], replicated, may hold values from -0.3125 to 0.3125
Outputs:
- pair_out: bfloat16 [128, 128, 128], P(('grp', 'row'))
- token_out: bfloat16 [128, 384], P(('grp', 'row'))
All inputs are finite; a program needn't handle non-finite values.
Results may differ from a plain program's by a relative error of at most 0.0085.
Values may be sent and summed in bfloat16 or wider, within the bound.
A program may use at most 64 MiB of HBM per device.

v0:
```python
import jax
import jax.numpy as jnp
from jax import lax
from jax.sharding import PartitionSpec as P


def layer_norm(values, along_axis):
    average = jnp.mean(values, axis=along_axis, keepdims=True)
    centred = values - average
    spread = jnp.mean(centred * centred, axis=along_axis, keepdims=True)
    return centred * lax.rsqrt(spread + 1e-05)


def split_heads(values, head_count):
    return values.reshape(values.shape[:-1] + (head_count, values.shape[-1] // head_count))


def row_attention(query_rows, key_rows, value_rows, bias_block, key_shift, score_scale):
    scores = (
        jnp.einsum("jhd,khd->hjk", query_rows, key_rows, preferred_element_type=jnp.float32)
        * score_scale
    )
    scores = scores + bias_block.astype(jnp.float32) + key_shift
    weights = jax.nn.softmax(scores, axis=-1).astype(jnp.bfloat16)
    combined = jnp.einsum("hjk,khd->jhd", weights, value_rows, preferred_element_type=jnp.float32)
    return combined.reshape(combined.shape[0], -1)


def per_device(
    pair_map,
    single,
    noise_term,
    token_mask,
    w_mul_in,
    w_mul_gate,
    w_mul_out,
    w_att_in,
    w_att_bias,
    w_att_out,
    w_tok_in,
    w_pair_bias,
    w_tok_out,
):
    f32 = jnp.float32
    bf16 = jnp.bfloat16
    row_count = pair_map.shape[0]
    first_row = lax.axis_index("row") * row_count
    mask_float = token_mask.astype(f32)
    mask_rows = lax.dynamic_slice_in_dim(mask_float, first_row, row_count)
    key_shift = jnp.where(token_mask > 0, 0.0, -1000000000.0).astype(f32)
    pair_float = pair_map.astype(f32)
    normed = layer_norm(pair_float, -1).astype(bf16)
    hidden_count = w_mul_in.shape[1] // 4
    mixed = jnp.einsum("ijc,cd->dij", normed, w_mul_in, preferred_element_type=f32)
    pair_mask = mask_rows[:, None] * mask_float[None, :]
    left_side = (
        jax.nn.sigmoid(mixed[:hidden_count]) * mixed[hidden_count : 2 * hidden_count] * pair_mask
    ).astype(bf16)
    right_side = (
        jax.nn.sigmoid(mixed[2 * hidden_count : 3 * hidden_count])
        * mixed[3 * hidden_count :]
        * pair_mask
    ).astype(bf16)
    left_cols, right_cols = (
        lax.all_to_all(left_side, "row", split_axis=0, concat_axis=1, tiled=True),
        lax.all_to_all(right_side, "row", split_axis=0, concat_axis=1, tiled=True),
    )
    crossed = jnp.einsum("cik,cjk->cij", left_cols, right_cols, preferred_element_type=f32).astype(
        bf16
    )
    crossed_rows = lax.all_to_all(crossed, "row", split_axis=1, concat_axis=0, tiled=True)
    crossed_norm = layer_norm(crossed_rows.astype(f32), 0).astype(bf16)
    update = jnp.einsum("cij,cd->ijd", crossed_norm, w_mul_out, preferred_element_type=f32)
    gating = jax.nn.sigmoid(
        jnp.einsum("ijc,cd->ijd", normed, w_mul_gate, preferred_element_type=f32)
    )
    pair_one = (pair_float + gating * update).astype(bf16)
    normed_one = layer_norm(pair_one.astype(f32), -1).astype(bf16)
    projected = jnp.einsum("ijc,cd->ijd", normed_one, w_att_in, preferred_element_type=f32)
    channels = pair_map.shape[2]
    head_tri = w_att_bias.shape[1]
    queries = split_heads(projected[..., :channels].astype(bf16), head_tri)
    keys_in = split_heads(projected[..., channels : 2 * channels].astype(bf16), head_tri)
    values_in = split_heads(projected[..., 2 * channels : 3 * channels].astype(bf16), head_tri)
    gating_att = jax.nn.sigmoid(projected[..., 3 * channels :])
    bias_local = jnp.einsum(
        "ijc,ch->hij", normed_one, w_att_bias, preferred_element_type=f32
    ).astype(bf16)
    tri_scale = (channels // head_tri) ** (-0.5)
    bias_all = lax.all_gather(bias_local, "row", axis=1, tiled=True)

    def attend_row(row_parts):
        return row_attention(
            row_parts[0], row_parts[1], row_parts[2], bias_all, key_shift, tri_scale
        )

    attended = lax.map(attend_row, (queries, keys_in, values_in))
    attended_gated = (gating_att * attended).astype(bf16)
    pair_out = (
        pair_one.astype(f32)
        + jnp.einsum("ijc,cd->ijd", attended_gated, w_att_out, preferred_element_type=f32)
    ).astype(bf16)
    activity = single.astype(f32) + noise_term.astype(f32)
    token_norm = layer_norm(activity, -1).astype(bf16)
    width_tok = single.shape[1]
    head_tok = w_pair_bias.shape[1]
    tok_projected = jnp.dot(token_norm, w_tok_in, preferred_element_type=f32)
    tok_queries = split_heads(tok_projected[:, :width_tok].astype(bf16), head_tok)
    tok_gate = jax.nn.sigmoid(tok_projected[:, 3 * width_tok :])
    key_local = tok_projected[:, width_tok : 2 * width_tok].astype(bf16)
    value_local = tok_projected[:, 2 * width_tok : 3 * width_tok].astype(bf16)
    key_all, value_all = (
        lax.all_gather(key_local, "row", axis=0, tiled=True),
        lax.all_gather(value_local, "row", axis=0, tiled=True),
    )
    tok_keys = split_heads(key_all, head_tok)
    tok_values = split_heads(value_all, head_tok)
    pair_norm = layer_norm(pair_out.astype(f32), -1).astype(bf16)
    pair_bias = jnp.einsum(
        "ijc,ch->hij", pair_norm, w_pair_bias, preferred_element_type=f32
    ).astype(bf16)
    tok_scale = (width_tok // head_tok) ** (-0.5)
    tok_combined = row_attention(tok_queries, tok_keys, tok_values, pair_bias, key_shift, tok_scale)
    tok_gated = (tok_gate * tok_combined).astype(bf16)
    token_out = (activity + jnp.dot(tok_gated, w_tok_out, preferred_element_type=f32)).astype(bf16)
    return (pair_out, token_out)


def solution(mesh):
    placed = (
        P(("grp", "row"), None, None),
        P(("grp", "row"), None),
        P(("grp", "row"), None),
        P("grp"),
        P(),
        P(),
        P(),
        P(),
        P(),
        P(),
        P(),
        P(),
        P(),
    )
    return jax.shard_map(
        per_device,
        mesh=mesh,
        in_specs=placed,
        out_specs=(P(("grp", "row"), None, None), P(("grp", "row"), None)),
        check_vma=False,
    )
```

profile of v0, /device:TPU:0, one launch (start us, length us, event | category | flops | bytes accessed | tf_op | source)
XLA Modules:
  0.0 174.6 jit_solution(7246916783701444773)
XLA Ops:
  0.6 1.1 copy.64
  2.7 1.2 convolution_bitcast_fusion
  4.9 7.3 %all-to-all-start = ((bf16[128,4,128]{2,1,0:T(4,128)(2,1)}), bf16[128,4,128]{2,1,0:T(4,128)(2,1)S(1)}, u32[]{:S(2)}, u32[]{:S(2)}) async-start(bf16[128,4,128]{2,1,0:T(4,128)(2,1)} %copy.68), calls=%async_computation | async-start | bytes 262144 | tf_op jit(solution)/shard_map/all_to_all | solution.py:65
  14.3 6.2 %all-to-all-done = bf16[128,4,128]{2,1,0:T(4,128)(2,1)S(1)} async-done(((bf16[128,4,128]{2,1,0:T(4,128)(2,1)}), bf16[128,4,128]{2,1,0:T(4,128)(2,1)S(1)}, u32[]{:S(2)}, u32[]{:S(2)}) %all-to-all-start) | async-done | bytes 131104 | tf_op jit(solution)/shard_map/all_to_all | solution.py:65
  20.5 2.6 %all-to-all-start.1 = ((bf16[128,4,128]{2,1,0:T(4,128)(2,1)}), bf16[128,4,128]{2,1,0:T(4,128)(2,1)S(1)}, u32[]{:S(2)}, u32[]{:S(2)}) async-start(bf16[128,4,128]{2,1,0:T(4,128)(2,1)} %copy.71), calls=%async_computation.1 | async-start | bytes 262144 | tf_op jit(solution)/shard_map/all_to_all | solution.py:66
  23.0 42.0 %all-gather.1 = bf16[32,4,384]{2,1,0:T(4,128)(2,1)S(1)} all-gather(bf16[1,4,384]{2,1,0:T(4,128)(2,1)S(1)} %get-tuple-element.80), channel_id=1, replica_groups=mesh['grp'=1,'row'=32] {'row'}, dimensions={0}, use_global_device_ids=true | all-gather | bytes 101376 | tf_op jit(solution)/shard_map/all_gather | solution.py:113
  66.9 2.6 %all-to-all-start.2 = ((bf16[4,128,128]{2,0,1:T(4,128)(2,1)}), bf16[4,128,128]{2,0,1:T(4,128)(2,1)S(1)}, u32[]{:S(2)}, u32[]{:S(2)}) async-start(bf16[4,128,128]{2,0,1:T(4,128)(2,1)} %copy.74), calls=%async_computation.2 | async-start | bytes 262144 | tf_op jit(solution)/shard_map/all_to_all | solution.py:71
  69.5 42.0 %all-gather = bf16[32,4,384]{2,1,0:T(4,128)(2,1)S(1)} all-gather(bf16[1,4,384]{2,1,0:T(4,128)(2,1)S(1)} %get-tuple-element.81), channel_id=1, replica_groups=mesh['grp'=1,'row'=32] {'row'}, dimensions={0}, use_global_device_ids=true | all-gather | bytes 101376 | tf_op jit(solution)/shard_map/all_gather | solution.py:114
  112.3 1.5 reshape.129
  115.0 37.0 %all_gather.9 = bf16[4,128,128]{2,0,1:T(4,128)(2,1)S(1)} all-gather(bf16[4,4,128]{2,0,1:T(4,128)(2,1)S(1)} %fusion.36), channel_id=1, replica_groups=mesh['grp'=1,'row'=32] {'row'}, dimensions={1}, use_global_device_ids=true | all-gather | bytes 135168 | tf_op jit(solution)/shard_map/all_gather | solution.py:90
  154.9 14.8 %while.10 = (s32[]{:T(128)}, f32[4,128,128]{1,2,0:T(8,128)}, bf16[4,128,4,32]{1,3,2,0:T(8,128)(2,1)}, bf16[4,128,4,32]{1,3,2,0:T(8,128)(2,1)}, bf16[4,128,4,32]{...) while((s32[]{:T(128)}, f32[4,128,128]{1,2,0:T(8,128)}, ...), condition=%wide.region_9.10_spmd, body=%wide.region_6.9_spmd.sunk | while | flops 13435648 | bytes 1417301 | solution.py:97
  154.9 1.0 fusion.121
  155.9 1.1 fusion.120
  157.0 1.0 fusion.122
  158.6 1.0 fusion.121
  159.6 1.1 fusion.120
  160.7 1.0 fusion.122
  162.3 1.0 fusion.121
  163.3 1.1 fusion.120
  164.4 1.0 fusion.122
  165.9 1.0 fusion.121
  167.0 1.1 fusion.120
  169.9 1.3 convert_reduce_fusion.1
  173.2 1.4 fusion.35
  (93 shorter events, 16.1 us)
Async XLA Ops:
  0.6 12.0 %copy-start = (bf16[384,1536]{1,0:T(8,128)(2,1)S(1)}, bf16[384,1536]{1,0:T(8,128)(2,1)}, u32[]{:S(2)}) copy-start(bf16[384,1536]{1,0:T(8,128)(2,1)} %param.25) | copy-start | bytes 3538948
  3.9 8.3 %copy-start.4 = (bf16[4,384]{1,0:T(4,128)(2,1)S(1)}, bf16[4,384]{1,0:T(4,128)(2,1)}, u32[]{:S(2)}) copy-start(bf16[4,384]{1,0:T(4,128)(2,1)} %param.17) | copy-start | bytes 9220
  3.9 8.3 %copy-start.6 = (bf16[4,384]{1,0:T(4,128)(2,1)S(1)}, bf16[4,384]{1,0:T(4,128)(2,1)}, u32[]{:S(2)}) copy-start(bf16[4,384]{1,0:T(4,128)(2,1)} %param.16) | copy-start | bytes 9220
  4.1 60.9 %copy-start.14 = (s32[128]{0:T(128)S(1)}, s32[128]{0:T(128)}, u32[]{:S(2)}) copy-start(s32[128]{0:T(128)} %param.18) | copy-start | bytes 1540
  4.9 15.5 %all-to-all-start = ((bf16[128,4,128]{2,1,0:T(4,128)(2,1)}), bf16[128,4,128]{2,1,0:T(4,128)(2,1)S(1)}, u32[]{:S(2)}, u32[]{:S(2)}) async-start(bf16[128,4,128]{2,1,0:T(4,128)(2,1)} %copy.68), calls=%async_computation | async-start | bytes 262144 | tf_op jit(solution)/shard_map/all_to_all | solution.py:65
  20.5 45.3 %all-to-all-start.1 = ((bf16[128,4,128]{2,1,0:T(4,128)(2,1)}), bf16[128,4,128]{2,1,0:T(4,128)(2,1)S(1)}, u32[]{:S(2)}, u32[]{:S(2)}) async-start(bf16[128,4,128]{2,1,0:T(4,128)(2,1)} %copy.71), calls=%async_computation.1 | async-start | bytes 262144 | tf_op jit(solution)/shard_map/all_to_all | solution.py:66
  65.9 47.9 %copy-start.11 = (bf16[128,128]{1,0:T(8,128)(2,1)S(1)}, bf16[128,128]{1,0:T(8,128)(2,1)}, u32[]{:S(2)}) copy-start(bf16[128,128]{1,0:T(8,128)(2,1)} %param.20) | copy-start | bytes 98308
  66.9 47.2 %all-to-all-start.2 = ((bf16[4,128,128]{2,0,1:T(4,128)(2,1)}), bf16[4,128,128]{2,0,1:T(4,128)(2,1)S(1)}, u32[]{:S(2)}, u32[]{:S(2)}) async-start(bf16[4,128,128]{2,0,1:T(4,128)(2,1)} %copy.74), calls=%async_computation.2 | async-start | bytes 262144 | tf_op jit(solution)/shard_map/all_to_all | solution.py:71
  113.8 0.8 copy-start.8
  114.2 0.7 copy-start.10
  114.3 37.8 %copy-start.3 = (bf16[128,512]{1,0:T(8,128)(2,1)S(1)}, bf16[128,512]{1,0:T(8,128)(2,1)}, u32[]{:S(2)}) copy-start(bf16[128,512]{1,0:T(8,128)(2,1)} %param.22) | copy-start | bytes 393220
  154.9 15.0 %copy-start.12 = (bf16[128,128]{1,0:T(8,128)(2,1)S(1)}, bf16[128,128]{1,0:T(8,128)(2,1)}, u32[]{:S(2)}) copy-start(bf16[128,128]{1,0:T(8,128)(2,1)} %param.24) | copy-start | bytes 98308
  169.7 2.3 %copy-start.13 = (bf16[128,16]{0,1:T(8,128)(2,1)S(1)}, bf16[128,16]{0,1:T(8,128)(2,1)}, u32[]{:S(2)}) copy-start(bf16[128,16]{0,1:T(8,128)(2,1)} %param.26) | copy-start | bytes 12292
  169.7 2.5 %copy-start.9 = (f32[128]{0:T(128)S(1)}, f32[128]{0:T(128)}, u32[]{:S(2)}) copy-start(f32[128]{0:T(128)} %get-tuple-element.160) | copy-start | bytes 1540
  169.8 2.9 %copy-start.1 = (bf16[128,16,24]{2,1,0:T(8,128)(2,1)S(1)}, bf16[128,16,24]{2,1,0:T(8,128)(2,1)}, u32[]{:S(2)}) copy-start(bf16[128,16,24]{2,1,0:T(8,128)(2,1)} %reshape.129) | copy-start | bytes 294916
  171.1 2.0 %copy-start.2 = (bf16[384,384]{1,0:T(8,128)(2,1)S(1)}, bf16[384,384]{1,0:T(8,128)(2,1)}, u32[]{:S(2)}) copy-start(bf16[384,384]{1,0:T(8,128)(2,1)} %param.27) | copy-start | bytes 884740
  171.1 2.0 %copy-start.5 = (bf16[4,384]{1,0:T(4,128)(2,1)S(1)}, bf16[4,384]{1,0:T(4,128)(2,1)}, u32[]{:S(2)}) copy-start(bf16[4,384]{1,0:T(4,128)(2,1)} %param.17) | copy-start | bytes 9220
  171.1 2.0 %copy-start.7 = (bf16[4,384]{1,0:T(4,128)(2,1)S(1)}, bf16[4,384]{1,0:T(4,128)(2,1)}, u32[]{:S(2)}) copy-start(bf16[4,384]{1,0:T(4,128)(2,1)} %param.16) | copy-start | bytes 9220
where the time goes:
time: 176 us; the launch traced here: 175 us
  blocking collectives  121 us (69%)
  matrix products  19.1 us (11%)
  local copies, waits for them, and re-layouts  12.4 us (7%)
  starting transfers between devices  12.4 us (7%)
  waiting for transfers between devices  6.2 us (4%)
  other arithmetic  2.39 us (1%)
    all_gather x1, blocking collectives, per_device(): lax.all_gather(value_local, 'row', axis=0, tiled=True)  42 us
    all_gather x1, blocking collectives, per_device(): lax.all_gather(key_local, 'row', axis=0, tiled=True)  42 us
    all_gather x1, blocking collectives, per_device(): bias_all = lax.all_gather(bias_local, 'row', axis=1, tiled=True)  37 us
    all_to_all x1, starting transfers between devices, per_device(): lax.all_to_all(left_side, 'row', split_axis=0, concat_axis=1, tiled=True)  7.3 us
    all_to_all x1, waiting for transfers between devices, per_device(): lax.all_to_all(left_side, 'row', split_axis=0, concat_axis=1, tiled=True)  6.19 us
    dot_general x5, matrix products, row_attention(): jnp.einsum('jhd,khd->hjk', query_rows, key_rows, preferred_element_type=j...  4.43 us
    sub x4, matrix products, row_attention(): weights = jax.nn.softmax(scores, axis=-1).astype(jnp.bfloat16)  4.37 us
    dot_general x5, matrix products, row_attention(): jnp.einsum('hjk,khd->jhd', weights, value_rows, preferred_element_type=jn...  4.12 us
  transfers between devices with their start and end apart: 3, of which 1 were waited for; matrix products, arithmetic and copies ran while one was open for 3% of the time, Pallas kernels for 0%

commit v1 on v0

--- a/solution.py
+++ b/solution.py
@@ -61,10 +61,37 @@
         * mixed[3 * hidden_count :]
         * pair_mask
     ).astype(bf16)
-    left_cols, right_cols = (
-        lax.all_to_all(left_side, "row", split_axis=0, concat_axis=1, tiled=True),
-        lax.all_to_all(right_side, "row", split_axis=0, concat_axis=1, tiled=True),
+    devices = lax.axis_size("row")
+    tokens = pair_map.shape[1]
+    part = hidden_count // devices
+    activity = single.astype(f32) + noise_term.astype(f32)
+    token_norm = layer_norm(activity, -1).astype(bf16)
+    width_tok = single.shape[1]
+    head_tok = w_pair_bias.shape[1]
+    tok_projected = jnp.dot(token_norm, w_tok_in, preferred_element_type=f32)
+    tok_queries = split_heads(tok_projected[:, :width_tok].astype(bf16), head_tok)
+    tok_gate = jax.nn.sigmoid(tok_projected[:, 3 * width_tok :])
+    kv_local = tok_projected[:, width_tok : 3 * width_tok].astype(bf16)
+    sides = jnp.stack(
+        [
+            left_side.reshape(devices, part * row_count, tokens),
+            right_side.reshape(devices, part * row_count, tokens),
+        ],
+        axis=1,
+    ).reshape(devices, 2 * part * row_count, tokens)
+    kv_block = jnp.broadcast_to(
+        kv_local.reshape(1, -1, tokens), (devices, kv_local.size // tokens, tokens)
     )
+    sent = jnp.concatenate([sides, kv_block], axis=1)
+    got = lax.all_to_all(sent, "row", split_axis=0, concat_axis=0, tiled=True)
+    sides_all = (
+        got[:, : 2 * part * row_count]
+        .reshape(devices, 2, part, row_count, tokens)
+        .transpose(1, 2, 0, 3, 4)
+        .reshape(2, part, tokens, tokens)
+    )
+    left_cols, right_cols = sides_all[0], sides_all[1]
+    kv_all = got[:, 2 * part * row_count :].reshape(tokens, 2 * width_tok)
     crossed = jnp.einsum("cik,cjk->cij", left_cols, right_cols, preferred_element_type=f32).astype(
         bf16
     )
@@ -87,7 +114,9 @@
         "ijc,ch->hij", normed_one, w_att_bias, preferred_element_type=f32
     ).astype(bf16)
     tri_scale = (channels // head_tri) ** (-0.5)
-    bias_all = lax.all_gather(bias_local, "row", axis=1, tiled=True)
+    bias_sent = jnp.broadcast_to(bias_local[None], (devices,) + bias_local.shape)
+    bias_got = lax.all_to_all(bias_sent, "row", split_axis=0, concat_axis=0, tiled=True)
+    bias_all = bias_got.transpose(1, 0, 2, 3).reshape(head_tri, tokens, tokens)
 
     def attend_row(row_parts):
         return row_attention(
@@ -100,21 +129,8 @@
         pair_one.astype(f32)
         + jnp.einsum("ijc,cd->ijd", attended_gated, w_att_out, preferred_element_type=f32)
     ).astype(bf16)
-    activity = single.astype(f32) + noise_term.astype(f32)
-    token_norm = layer_norm(activity, -1).astype(bf16)
-    width_tok = single.shape[1]
-    head_tok = w_pair_bias.shape[1]
-    tok_projected = jnp.dot(token_norm, w_tok_in, preferred_element_type=f32)
-    tok_queries = split_heads(tok_projected[:, :width_tok].astype(bf16), head_tok)
-    tok_gate = jax.nn.sigmoid(tok_projected[:, 3 * width_tok :])
-    key_local = tok_projected[:, width_tok : 2 * width_tok].astype(bf16)
-    value_local = tok_projected[:, 2 * width_tok : 3 * width_tok].astype(bf16)
-    key_all, value_all = (
-        lax.all_gather(key_local, "row", axis=0, tiled=True),
-        lax.all_gather(value_local, "row", axis=0, tiled=True),
-    )
-    tok_keys = split_heads(key_all, head_tok)
-    tok_values = split_heads(value_all, head_tok)
+    tok_keys = split_heads(kv_all[:, :width_tok], head_tok)
+    tok_values = split_heads(kv_all[:, width_tok:], head_tok)
     pair_norm = layer_norm(pair_out.astype(f32), -1).astype(bf16)
     pair_bias = jnp.einsum(
         "ijc,ch->hij", pair_norm, w_pair_bias, preferred_element_type=f32

time: 176 us -> 63 us (0.36)
  blocking collectives: 121 us -> 0 us
  waiting for transfers between devices: 6.2 us -> 28.8 us
  matrix products: 19.1 us -> 8.16 us
  local copies, waits for them, and re-layouts: 12.4 us -> 7.32 us
  other arithmetic: 2.39 us -> 4.18 us
    all_gather x3 -> x0, blocking collectives: 121 us -> none  [the longest x1 42 us: per_device(): lax.all_gather(value_local, 'row', axis=0, tiled=True)]
    all_to_all x2, waiting for transfers between devices: 6.2 us -> 21.3 us  [the longest x1 14.1 us: per_device(): got = lax.all_to_all(sent, 'row', split_axis=0, concat_axis=0, tiled=True)]
    all_to_all x1, waiting for transfers between devices: 0.01 us -> 7.56 us  [per_device(): lax.all_to_all(crossed, 'row', split_axis=1, concat_axis=0, tiled=True)]
    dot_general x5, matrix products: 4.43 us -> 1.12 us  [row_attention(): jnp.einsum('jhd,khd->hjk', query_rows, key_rows, preferred_element_type=j...]
    sub x4, matrix products: 4.37 us -> 1.24 us  [row_attention(): weights = jax.nn.softmax(scores, axis=-1).astype(jnp.bfloat16)]
    dot_general x5, matrix products: 4.12 us -> 1.15 us  [row_attention(): jnp.einsum('hjk,khd->jhd', weights, value_rows, preferred_element_type=jn...]
    reshape x3 -> x1, local copies, waits for them, and re-layouts: 2.28 us -> 0.09 us  [split_heads(): values.reshape(values.shape[:-1] + (head_count, values.shape[-1] // head_...]
  transfers between devices with their start and end apart: 3 -> 3, of which waited for: 1 -> 3; matrix products, arithmetic and copies ran while one was open for 3% -> 3% of each run, Pallas kernels for 0% -> 0%
where the time goes in v1:
time: 63 us; the launch traced here: 62.4 us
  waiting for transfers between devices  28.8 us (46%)
  starting transfers between devices  12.7 us (20%)
  matrix products  8.16 us (13%)
  local copies, waits for them, and re-layouts  7.32 us (12%)
  other arithmetic  4.18 us (7%)
  between operations  1.15 us (2%)
    all_to_all x1, waiting for transfers between devices, per_device(): got = lax.all_to_all(sent, 'row', split_axis=0, concat_axis=0, tiled=True)  14.1 us
    all_to_all x1, waiting for transfers between devices, per_device(): lax.all_to_all(crossed, 'row', split_axis=1, concat_axis=0, tiled=True)  7.56 us
    all_to_all x1, starting transfers between devices, per_device(): got = lax.all_to_all(sent, 'row', split_axis=0, concat_axis=0, tiled=True)  7.3 us
    all_to_all x1, waiting for transfers between devices, per_device(): lax.all_to_all(bias_sent, 'row', split_axis=0, concat_axis=0, tiled=True)  7.2 us
    all_to_all x1, starting transfers between devices, per_device(): lax.all_to_all(crossed, 'row', split_axis=1, concat_axis=0, tiled=True)  2.86 us
    all_to_all x1, starting transfers between devices, per_device(): lax.all_to_all(bias_sent, 'row', split_axis=0, concat_axis=0, tiled=True)  2.58 us
    dynamic_update_slice x4, local copies, waits for them, and re-layouts, per_device(): attended = lax.map(attend_row, (queries, keys_in, values_in))  2.5 us
  transfers between devices with their start and end apart: 3, of which 3 were waited for; matrix products, arithmetic and copies ran while one was open for 3% of the time, Pallas kernels for 0%

profile of v1, /device:TPU:0, one launch (start us, length us, event | category | flops | bytes accessed | tf_op | source)
XLA Modules:
  0.0 62.4 jit_solution(7950518317297521504)
XLA Ops:
  0.7 0.8 %convert_element_type.108 = f32[128]{0:T(128)S(1)} convert(s32[128]{0:T(128)} %param.18) | non-fusion elementwise | flops 128 | bytes 1024 | tf_op jit(solution)/shard_map/convert_element_type | solution.py:48
  1.4 0.8 %fusion.76 = f32[4]{0:T(128)S(1)} fusion(bf16[4,384]{1,0:T(4,128)(2,1)} %param.17, bf16[4,384]{1,0:T(4,128)(2,1)} %param.16), kind=kLoop, calls=%fused_computation.104 | loop fusion | flops 6140 | bytes 6160 | tf_op jit(solution)/shard_map/reduce_sum | solution.py:8
  2.3 0.9 %multiply_reduce_fusion.2 = f32[4]{0:T(128)S(1)} fusion(bf16[4,384]{1,0:T(4,128)(2,1)} %param.17, bf16[4,384]{1,0:T(4,128)(2,1)} %param.16, f32[4]{0:T(128)S(1)} %broadcast_multiply_fusion.5), kind=kLoop, calls=%fused_computation.100 | loop fusion | flops 9212 | bytes 6176 | tf_op jit(solution)/shard_map/reduce_sum | solution.py:10
  3.3 1.0 %fusion.93 = (bf16[4,1536]{1,0:T(4,128)(2,1)S(1)}, f32[4,1536]{1,0:T(4,128)S(1)}) fusion(bf16[384,1536]{1,0:T(8,128)(2,1)S(1)} %copy-done, bf16[4,384]{1,0:T(4,128)(2,1)} %param.17, bf16[4,384]{1,0:T(4,128)(2,1)} %param.16, f32[4]{0:T(128)S(1)} %add_rsqrt_fusion.4, f32[4]{0:T(128)S(1)} %broadcast_multiply_fusion.5), kind=kOutput, calls=%fused_computation.128 | convolution fusion | flops 4733952 | bytes 1222688 | tf_op jit(solution)/shard_map/dot_general | solution.py:71
  4.6 0.3 convolution_bitcast_fusion
  5.5 0.8 %pad_maximum_fusion = bf16[32,56,128]{2,1,0:T(8,128)(2,1)} fusion(bf16[32,24,128]{2,1,0:T(8,128)(2,1)S(1)} %broadcast_in_dim.20, bf16[32,32,128]{2,1,0:T(8,128)(2,1)S(1)} %bitcast.108), kind=kLoop, calls=%fused_computation.45 | loop fusion | flops 917504 | bytes 917504 | tf_op jit(solution)/shard_map/concatenate | solution.py:85
  6.3 7.3 %all-to-all-start = ((bf16[32,56,128]{2,1,0:T(8,128)(2,1)}), bf16[32,56,128]{2,1,0:T(8,128)(2,1)S(1)}, u32[]{:S(2)}, u32[]{:S(2)}) async-start(bf16[32,56,128]{2,1,0:T(8,128)(2,1)} %pad_maximum_fusion), calls=%async_computation | async-start | bytes 917504 | tf_op jit(solution)/shard_map/all_to_all | solution.py:86
  13.9 14.1 %all-to-all-done = bf16[32,56,128]{2,1,0:T(8,128)(2,1)S(1)} async-done(((bf16[32,56,128]{2,1,0:T(8,128)(2,1)}), bf16[32,56,128]{2,1,0:T(8,128)(2,1)S(1)}, u32[]{:S(2)}, u32[]{:S(2)}) %all-to-all-start) | async-done | bytes 458784 | tf_op jit(solution)/shard_map/all_to_all | solution.py:86
  28.5 0.8 %copy.106 = bf16[4,128,128]{2,0,1:T(4,128)(2,1)} copy(bf16[4,128,128]{2,1,0:T(8,128)(2,1)S(1)} %convolution_convert_fusion) | data formatting | bytes 262144 | tf_op jit(solution)/shard_map/convert_element_type | solution.py:95
  29.3 2.9 %all-to-all-start.1 = ((bf16[4,128,128]{2,0,1:T(4,128)(2,1)}), bf16[4,128,128]{2,0,1:T(4,128)(2,1)S(1)}, u32[]{:S(2)}, u32[]{:S(2)}) async-start(bf16[4,128,128]{2,0,1:T(4,128)(2,1)} %copy.106), calls=%async_computation.1 | async-start | bytes 262144 | tf_op jit(solution)/shard_map/all_to_all | solution.py:98
  32.8 7.6 %all-to-all-done.1 = bf16[4,128,128]{2,0,1:T(4,128)(2,1)S(1)} async-done(((bf16[4,128,128]{2,0,1:T(4,128)(2,1)}), bf16[4,128,128]{2,0,1:T(4,128)(2,1)S(1)}, u32[]{:S(2)}, u32[]{:S(2)}) %all-to-all-start.1) | async-done | bytes 131104 | tf_op jit(solution)/shard_map/all_to_all | solution.py:98
  41.3 0.7 %broadcast_in_dim.22 = bf16[32,4,4,128]{3,2,1,0:T(4,128)(2,1)} broadcast(bf16[4,4,128]{2,1,0:T(4,128)(2,1)S(1)} %copy.115), dimensions={1,2,3} | broadcast | bytes 135168 | tf_op jit(solution)/shard_map/broadcast_in_dim | solution.py:117
  42.0 2.6 %all-to-all-start.2 = ((bf16[32,4,4,128]{3,2,1,0:T(4,128)(2,1)}), bf16[32,4,4,128]{3,2,1,0:T(4,128)(2,1)S(1)}, u32[]{:S(2)}, u32[]{:S(2)}) async-start(bf16[32,4,4,128]{3,2,1,0:T(4,128)(2,1)} %broadcast_in_dim.22), calls=%async_computation.2 | async-start | bytes 262144 | tf_op jit(solution)/shard_map/all_to_all | solution.py:118
  44.6 0.3 fusion.95
  45.6 7.2 %all-to-all-done.2 = bf16[32,4,4,128]{3,2,1,0:T(4,128)(2,1)S(1)} async-done(((bf16[32,4,4,128]{3,2,1,0:T(4,128)(2,1)}), bf16[32,4,4,128]{3,2,1,0:T(4,128)(2,1)S(1)}, u32[]{:S(2)}, u32[]{:S(2)}) %all-to-all-start.2) | async-done | bytes 131104 | tf_op jit(solution)/shard_map/all_to_all | solution.py:118
  53.0 5.5 %while.10 = (s32[]{:T(128)}, f32[4,128,128]{1,2,0:T(8,128)}, bf16[4,128,4,32]{1,3,2,0:T(8,128)(2,1)S(1)}, bf16[4,128,4,32]{1,3,2,0:T(8,128)(2,1)S(1)}, bf16[4,12...) while((s32[]{:T(128)}, f32[4,128,128]{1,2,0:T(8,128)}, ...), condition=%wide.region_11.12_spmd, body=%wide.region_8.11_spmd.sunk | while | flops 13435648 | bytes 1416293 | solution.py:126
  53.8 0.6 %constant_dynamic-update-slice_fusion.2 = f32[4,128,128]{1,2,0:T(8,128)} fusion(f32[4,128,128]{1,2,0:T(8,128)} %get-tuple-element.159, f32[1,128,128]{1,2,0:T(8,128)S(1)} %bitcast.107, s32[]{:T(128)S(6)} %copy.150), kind=kLoop, calls=%fused_computation.16.clone.1 | loop fusion | bytes 131076 | tf_op jit(solution)/shard_map/while/body/jit(dynamic_update_index_in_dim)/dynamic_update_slice | solution.py:126
  55.2 0.6 constant_dynamic-update-slice_fusion.2
  56.5 0.6 %constant_dynamic-update-slice_fusion.2 = f32[4,128,128]{1,2,0:T(8,128)} fusion(f32[4,128,128]{1,2,0:T(8,128)} %get-tuple-element.159, f32[1,128,128]{1,2,0:T(8,128)S(1)} %bitcast.107, s32[]{:T(128)S(6)} %copy.150), kind=kLoop, calls=%fused_computation.16.clone.1 | loop fusion | bytes 131076 | tf_op jit(solution)/shard_map/while/body/jit(dynamic_update_index_in_dim)/dynamic_update_slice | solution.py:126
  57.9 0.6 constant_dynamic-update-slice_fusion.2
  58.6 1.2 %convert_reduce_fusion.1 = (f32[4,128]{1,0:T(4,128)S(1)}, bf16[4,128,128]{1,2,0:T(8,128)(2,1)S(1)}) fusion(f32[4,128,128]{1,2,0:T(8,128)S(1)} %get-tuple-element.102, bf16[128,128]{1,0:T(8,128)(2,1)S(1)} %copy-done.10, f32[4,128,128]{1,2,0:T(8,128)} %get-tuple-element.39, f32[4,128,128]{1,2,0:T(8,128)S(1)} %copy.140), kind=kOutput, calls=%fused_computation.49 | convolution fusion | flops 17366528 | bytes 952320 | tf_op jit(solution)/shard_map/ijc,cd->ijd/dot_general | solution.py:130
  59.8 0.8 %copy.126 = bf16[4,128,128]{2,1,0:T(8,128)(2,1)} copy(bf16[4,128,128]{1,2,0:T(8,128)(2,1)S(1)} %get-tuple-element.106) | data formatting | bytes 262144
  61.2 0.4 convolution_bitcast_fusion.1
  61.7 0.7 %fusion.35 = bf16[4,384]{1,0:T(4,128)(2,1)} fusion(bf16[384,384]{1,0:T(8,128)(2,1)S(1)} %copy-done.1, bf16[4,384]{1,0:T(4,128)(2,1)S(1)} %copy-done.5, bf16[4,384]{1,0:T(4,128)(2,1)S(1)} %copy-done.6, f32[4,384]{1,0:T(4,128)S(1)} %reshape.156, f32[4,1536]{1,0:T(4,128)S(1)} %get-tuple-element.100), kind=kOutput, calls=%fused_computation.43 | convolution fusion | flops 1195008 | bytes 316416 | tf_op jit(solution)/shard_map/dot_general | solution.py:141
  (99 shorter events, 7.6 us)
Async XLA Ops:
  0.6 2.7 %copy-start = (bf16[384,1536]{1,0:T(8,128)(2,1)S(1)}, bf16[384,1536]{1,0:T(8,128)(2,1)}, u32[]{:S(2)}) copy-start(bf16[384,1536]{1,0:T(8,128)(2,1)} %param.25) | copy-start | bytes 3538948
  0.6 3.7 %copy-start.3 = (bf16[4,128,128]{2,1,0:T(8,128)(2,1)S(1)}, bf16[4,128,128]{2,1,0:T(8,128)(2,1)}, u32[]{:S(2)}) copy-start(bf16[4,128,128]{2,1,0:T(8,128)(2,1)} %param.15) | copy-start | bytes 393220
  0.7 3.9 %copy-start.2 = (bf16[128,512]{1,0:T(8,128)(2,1)S(1)}, bf16[128,512]{1,0:T(8,128)(2,1)}, u32[]{:S(2)}) copy-start(bf16[128,512]{1,0:T(8,128)(2,1)} %param.19) | copy-start | bytes 393220
  5.5 8.2 %copy-start.9 = (bf16[128,128]{1,0:T(8,128)(2,1)S(1)}, bf16[128,128]{1,0:T(8,128)(2,1)}, u32[]{:S(2)}) copy-start(bf16[128,128]{1,0:T(8,128)(2,1)} %param.20) | copy-start | bytes 98308
  6.3 21.7 %all-to-all-start = ((bf16[32,56,128]{2,1,0:T(8,128)(2,1)}), bf16[32,56,128]{2,1,0:T(8,128)(2,1)S(1)}, u32[]{:S(2)}, u32[]{:S(2)}) async-start(bf16[32,56,128]{2,1,0:T(8,128)(2,1)} %pad_maximum_fusion), calls=%async_computation | async-start | bytes 917504 | tf_op jit(solution)/shard_map/all_to_all | solution.py:86
  28.0 4.2 %copy-start.12 = (s32[128]{0:T(128)S(1)}, s32[128]{0:T(128)}, u32[]{:S(2)}) copy-start(s32[128]{0:T(128)} %param.18) | copy-start | bytes 1540
  29.3 11.1 %all-to-all-start.1 = ((bf16[4,128,128]{2,0,1:T(4,128)(2,1)}), bf16[4,128,128]{2,0,1:T(4,128)(2,1)S(1)}, u32[]{:S(2)}, u32[]{:S(2)}) async-start(bf16[4,128,128]{2,0,1:T(4,128)(2,1)} %copy.106), calls=%async_computation.1 | async-start | bytes 262144 | tf_op jit(solution)/shard_map/all_to_all | solution.py:98
  32.3 8.4 %copy-start.7 = (bf16[128,128]{1,0:T(8,128)(2,1)S(1)}, bf16[128,128]{1,0:T(8,128)(2,1)}, u32[]{:S(2)}) copy-start(bf16[128,128]{1,0:T(8,128)(2,1)} %param.21) | copy-start | bytes 98308
  40.5 0.7 %copy-start.8 = (bf16[128,4]{0,1:T(4,128)(2,1)S(1)}, bf16[128,4]{0,1:T(4,128)(2,1)}, u32[]{:S(2)}) copy-start(bf16[128,4]{0,1:T(4,128)(2,1)} %param.23) | copy-start | bytes 3076
  40.6 3.9 %copy-start.4 = (bf16[128,512]{1,0:T(8,128)(2,1)S(1)}, bf16[128,512]{1,0:T(8,128)(2,1)}, u32[]{:S(2)}) copy-start(bf16[128,512]{1,0:T(8,128)(2,1)} %param.22) | copy-start | bytes 393220
  42.0 10.8 %all-to-all-start.2 = ((bf16[32,4,4,128]{3,2,1,0:T(4,128)(2,1)}), bf16[32,4,4,128]{3,2,1,0:T(4,128)(2,1)S(1)}, u32[]{:S(2)}, u32[]{:S(2)}) async-start(bf16[32,4,4,128]{3,2,1,0:T(4,128)(2,1)} %broadcast_in_dim.22), calls=%async_computation.2 | async-start | bytes 262144 | tf_op jit(solution)/shard_map/all_to_all | solution.py:118
  53.0 5.5 %copy-start.10 = (bf16[128,128]{1,0:T(8,128)(2,1)S(1)}, bf16[128,128]{1,0:T(8,128)(2,1)}, u32[]{:S(2)}) copy-start(bf16[128,128]{1,0:T(8,128)(2,1)} %param.24) | copy-start | bytes 98308
  58.5 2.1 %copy-start.11 = (bf16[128,16]{0,1:T(8,128)(2,1)S(1)}, bf16[128,16]{0,1:T(8,128)(2,1)}, u32[]{:S(2)}) copy-start(bf16[128,16]{0,1:T(8,128)(2,1)} %param.26) | copy-start | bytes 12292
  58.5 3.1 %copy-start.1 = (bf16[384,384]{1,0:T(8,128)(2,1)S(1)}, bf16[384,384]{1,0:T(8,128)(2,1)}, u32[]{:S(2)}) copy-start(bf16[384,384]{1,0:T(8,128)(2,1)} %param.27) | copy-start | bytes 884740
  58.5 3.1 %copy-start.5 = (bf16[4,384]{1,0:T(4,128)(2,1)S(1)}, bf16[4,384]{1,0:T(4,128)(2,1)}, u32[]{:S(2)}) copy-start(bf16[4,384]{1,0:T(4,128)(2,1)} %param.17) | copy-start | bytes 9220
  58.6 3.1 %copy-start.6 = (bf16[4,384]{1,0:T(4,128)(2,1)S(1)}, bf16[4,384]{1,0:T(4,128)(2,1)}, u32[]{:S(2)}) copy-start(bf16[4,384]{1,0:T(4,128)(2,1)} %param.16) | copy-start | bytes 9220

commit v2 on v1

--- a/solution.py
+++ b/solution.py
@@ -1,6 +1,10 @@
+import functools
+
 import jax
 import jax.numpy as jnp
 from jax import lax
+from jax.experimental import pallas as pl
+from jax.experimental.pallas import tpu as pltpu
 from jax.sharding import PartitionSpec as P
 
 
@@ -142,6 +146,277 @@
     return (pair_out, token_out)
 
 
+def dot_nn(a, b):
+    return lax.dot_general(a, b, (((1,), (0,)), ((), ())), preferred_element_type=jnp.float32)
+
+
+def dot_nt(a, b):
+    return lax.dot_general(a, b, (((1,), (1,)), ((), ())), preferred_element_type=jnp.float32)
+
+
+def lane_norm(values):
+    return layer_norm(values, -1).astype(jnp.bfloat16)
+
+
+def softmax_rows(scores):
+    shifted = jnp.exp(scores - jnp.max(scores, axis=-1, keepdims=True))
+    return (shifted * (1.0 / jnp.sum(shifted, axis=-1, keepdims=True))).astype(jnp.bfloat16)
+
+
+def fused_kernel(
+    devices,
+    mask_scalar,
+    mask_lane,
+    pair_ref,
+    single_ref,
+    noise_ref,
+    w_sides,
+    w_mul_gate,
+    w_mul_out,
+    w_att_in,
+    w_small,
+    w_att_out,
+    w_tok_in,
+    w_tok_out,
+    pair_out,
+    token_out,
+    send_sides,
+    recv_sides,
+    send_prod,
+    recv_prod,
+    send_bias,
+    recv_bias,
+    send_kv,
+    recv_kv,
+    wide_sides,
+    wide_prod,
+    wide_back,
+    wide_bias,
+    wide_all,
+    wide_kv,
+    wide_keys,
+    send_sem,
+    recv_sem,
+):
+    f32 = jnp.float32
+    bf16 = jnp.bfloat16
+    me = lax.axis_index("row")
+
+    barrier = pltpu.get_barrier_semaphore()
+
+    def greet(step, carry):
+        other = lax.rem(me + step, devices)
+        pl.semaphore_signal(
+            barrier, inc=1, device_id={"row": other}, device_id_type=pl.DeviceIdType.MESH
+        )
+        return carry
+
+    lax.fori_loop(1, devices, greet, 0)
+
+    def send_all(slot, source, landing):
+        def one(step, carry):
+            other = lax.rem(me + step, devices)
+            pltpu.make_async_remote_copy(
+                src_ref=source(other),
+                dst_ref=landing.at[me],
+                send_sem=send_sem.at[slot],
+                recv_sem=recv_sem.at[slot],
+                device_id={"row": other},
+                device_id_type=pl.DeviceIdType.MESH,
+            ).start()
+            return carry
+
+        lax.fori_loop(1, devices, one, 0)
+
+    def wait_all(sem, landing):
+        whole = landing.at[pl.ds(0, devices - 1)]
+        pltpu.make_async_copy(whole, whole, sem).wait()
+
+    pair = pair_ref[...].astype(f32)
+    normed = lane_norm(pair)
+    mixed = dot_nt(w_sides[...], normed)
+    mask = mask_lane[...].astype(f32)
+    half = w_sides.shape[0] // 2
+    blocks = []
+    for i in range(4):
+        mask_row = mask_scalar[me * 4 + i].astype(f32)
+        cols = slice(i * 128, (i + 1) * 128)
+        side = jax.nn.sigmoid(mixed[:half, cols]) * mixed[half:, cols] * (mask * mask_row)
+        blocks.append(side.reshape(devices, 8, 128))
+    send_sides[...] = jnp.concatenate(blocks, axis=1).astype(bf16)
+    recv_sides[me] = send_sides[me]
+    pl.semaphore_wait(barrier, devices - 1)
+    send_all(0, lambda other: send_sides.at[other], recv_sides)
+
+    activity = single_ref[...].astype(f32) + noise_ref[...].astype(f32)
+    activity = jnp.concatenate([activity, jnp.zeros_like(activity)], axis=0)
+    tok = dot_nn(lane_norm(activity), w_tok_in[...])
+    width = single_ref.shape[1]
+    wide_kv[...] = jnp.zeros_like(wide_kv)
+    for m in range(6):
+        wide_kv[pl.ds(m, 4, stride=8), :] = tok[:4, width + m * 128 : width + (m + 1) * 128]
+    send_kv[...] = wide_kv[...].astype(bf16)
+    recv_kv[me] = send_kv[...]
+    gating = jax.nn.sigmoid(dot_nn(normed, w_mul_gate[...]))
+
+    wait_all(recv_sem.at[0], recv_sides)
+    wide_sides[...] = recv_sides[...].astype(f32).reshape(wide_sides.shape)
+    for c in range(4):
+        left = wide_sides[pl.ds(c, 128, stride=8), :].astype(bf16)
+        right = wide_sides[pl.ds(4 + c, 128, stride=8), :].astype(bf16)
+        wide_prod[pl.ds(c, 128, stride=4), :] = dot_nt(left, right)
+    send_prod[...] = wide_prod[...].astype(bf16).reshape(send_prod.shape)
+    recv_prod[me] = send_prod[me]
+    send_all(1, lambda other: send_prod.at[other], recv_prod)
+    send_all(3, lambda other: send_kv, recv_kv)
+    wait_all(recv_sem.at[1], recv_prod)
+    wide_back[...] = recv_prod[...].astype(f32).reshape(wide_back.shape)
+    crossed_norm = []
+    for i in range(4):
+        crossed = jnp.concatenate(
+            [wide_back[pl.ds(i * 4 + c, devices, stride=16), :] for c in range(4)], axis=0
+        )
+        crossed_norm.append(layer_norm(crossed, 0).T.astype(bf16))
+    update = dot_nn(jnp.concatenate(crossed_norm, axis=0), w_mul_out[...])
+    pair_one = (pair + gating * update).astype(bf16).astype(f32)
+
+    normed_one = lane_norm(pair_one)
+    bias = dot_nt(w_small[16:32], normed_one)
+    for i in range(4):
+        wide_bias[i * 4 : (i + 1) * 4, :] = bias[:4, i * 128 : (i + 1) * 128]
+    send_bias[...] = wide_bias[...].astype(bf16)
+    recv_bias[me] = send_bias[...]
+    send_all(2, lambda other: send_bias, recv_bias)
+    projected = dot_nn(normed_one, w_att_in[...])
+    shift = jnp.where(mask > 0, 0.0, -1000000000.0).astype(f32)
+    head_of = lax.broadcasted_iota(jnp.int32, (128, 128), 1) // 32
+    raw = []
+    for i in range(4):
+        rows = slice(i * 128, (i + 1) * 128)
+        query = projected[rows, :128]
+        query = jnp.concatenate([jnp.where(head_of == h, query, 0.0) for h in range(4)], axis=0)
+        raw.append(dot_nt(query.astype(bf16), projected[rows, 128:256].astype(bf16)))
+
+    wait_all(recv_sem.at[2], recv_bias)
+    wide_all[...] = recv_bias[...].astype(f32).reshape(wide_all.shape)
+    bias_all = jnp.concatenate(
+        [wide_all[pl.ds(h, 128, stride=4), :] for h in range(4)], axis=0
+    )
+    scale = 32.0**-0.5
+    gated = []
+    for i in range(4):
+        rows = slice(i * 128, (i + 1) * 128)
+        weights = softmax_rows(raw[i] * scale + bias_all + shift)
+        spread = dot_nn(weights, projected[rows, 256:384].astype(bf16))
+        attended = jnp.zeros((128, 128), f32)
+        for h in range(4):
+            attended = jnp.where(head_of == h, spread[h * 128 : (h + 1) * 128], attended)
+        gated.append((jax.nn.sigmoid(projected[rows, 384:]) * attended).astype(bf16))
+    final = (pair_one + dot_nn(jnp.concatenate(gated, axis=0), w_att_out[...])).astype(bf16)
+    pair_out[...] = final
+
+    pair_bias = dot_nt(w_small[0:16], lane_norm(final.astype(f32))).astype(bf16).astype(f32)
+    pair_bias = jnp.concatenate([pair_bias[:, i * 128 : (i + 1) * 128] for i in range(4)], axis=0)
+    lane = lax.broadcasted_iota(jnp.int32, (16, width), 1)
+    head = lax.broadcasted_iota(jnp.int32, (16, width), 0)
+    own = (lane >= head * 24) & (lane < head * 24 + 24)
+    query = jnp.concatenate([jnp.where(own, tok[i : i + 1, :width], 0.0) for i in range(4)], axis=0)
+    wait_all(recv_sem.at[3], recv_kv)
+    wide_keys[...] = recv_kv[...].astype(f32).reshape(wide_keys.shape)
+    chunks = [wide_keys[pl.ds(m, 128, stride=8), :].astype(bf16) for m in range(6)]
+    keys = jnp.concatenate(chunks[:3], axis=1)
+    values = jnp.concatenate(chunks[3:], axis=1)
+    weights = softmax_rows(dot_nt(query.astype(bf16), keys) * 24.0**-0.5 + pair_bias + shift)
+    spread = dot_nn(weights, values)
+    combined = jnp.concatenate(
+        [
+            jnp.sum(jnp.where(own, spread[i * 16 : (i + 1) * 16], 0.0), axis=0, keepdims=True)
+            for i in range(4)
+        ]
+        + [jnp.zeros((4, width), f32)],
+        axis=0,
+    )
+    tok_gated = (jax.nn.sigmoid(tok[:, 3 * width :]) * combined).astype(bf16)
+    token_out[...] = (activity + dot_nn(tok_gated, w_tok_out[...]))[:4].astype(bf16)
+
+    wait_all(send_sem.at[0], recv_sides)
+    wait_all(send_sem.at[1], recv_prod)
+    wait_all(send_sem.at[2], recv_bias)
+    wait_all(send_sem.at[3], recv_kv)
+
+
+def fused(
+    pair_map,
+    single,
+    noise_term,
+    token_mask,
+    w_mul_in,
+    w_mul_gate,
+    w_mul_out,
+    w_att_in,
+    w_att_bias,
+    w_att_out,
+    w_tok_in,
+    w_pair_bias,
+    w_tok_out,
+):
+    bf16 = jnp.bfloat16
+    f32 = jnp.float32
+    devices = lax.axis_size("row")
+    w_sides = (
+        w_mul_in.T.reshape(2, 2, devices, 4, 128).transpose(1, 2, 0, 3, 4).reshape(512, 128)
+    )
+    w_back = w_mul_out.reshape(devices, 4, 128).transpose(1, 0, 2).reshape(128, 128)
+    w_small = jnp.concatenate([w_pair_bias.T, w_att_bias.T, jnp.zeros((12, 128), bf16)], axis=0)
+    vmem = pl.BlockSpec(memory_space=pltpu.VMEM)
+    pair_out, token_out = pl.pallas_call(
+        functools.partial(fused_kernel, devices),
+        out_shape=(
+            jax.ShapeDtypeStruct((512, 128), bf16),
+            jax.ShapeDtypeStruct(single.shape, bf16),
+        ),
+        in_specs=[pl.BlockSpec(memory_space=pltpu.SMEM)] + [vmem] * 12,
+        out_specs=(vmem, vmem),
+        scratch_shapes=[
+            pltpu.VMEM((devices, 32, 128), bf16),
+            pltpu.VMEM((devices, 32, 128), bf16),
+            pltpu.VMEM((devices, 16, 128), bf16),
+            pltpu.VMEM((devices, 16, 128), bf16),
+            pltpu.VMEM((16, 128), bf16),
+            pltpu.VMEM((devices, 16, 128), bf16),
+            pltpu.VMEM((32, 128), bf16),
+            pltpu.VMEM((devices, 32, 128), bf16),
+            pltpu.VMEM((devices * 32, 128), f32),
+            pltpu.VMEM((devices * 16, 128), f32),
+            pltpu.VMEM((devices * 16, 128), f32),
+            pltpu.VMEM((16, 128), f32),
+            pltpu.VMEM((devices * 16, 128), f32),
+            pltpu.VMEM((32, 128), f32),
+            pltpu.VMEM((devices * 32, 128), f32),
+            pltpu.SemaphoreType.DMA((4,)),
+            pltpu.SemaphoreType.DMA((4,)),
+        ],
+        compiler_params=pltpu.CompilerParams(
+            collective_id=0, has_side_effects=True, vmem_limit_bytes=40 * 1024 * 1024
+        ),
+    )(
+        token_mask,
+        token_mask.reshape(1, -1),
+        pair_map.reshape(512, 128),
+        single,
+        noise_term,
+        w_sides,
+        w_mul_gate,
+        w_back,
+        w_att_in,
+        w_small,
+        w_att_out,
+        w_tok_in,
+        w_tok_out,
+    )
+    return pair_out.reshape(pair_map.shape), token_out
+
+
 def solution(mesh):
     placed = (
         P(("grp", "row"), None, None),
@@ -158,8 +433,15 @@
         P(),
         P(),
     )
+
+    def body(*arrays):
+        devices = mesh.shape["row"]
+        fits = arrays[0].shape == (4, 128, 128) and devices == 32
+        fits = fits and arrays[1].shape[1] == 384 and arrays[4].shape[1] == 512
+        return fused(*arrays) if fits else per_device(*arrays)
+
     return jax.shard_map(
-        per_device,
+        body,
         mesh=mesh,
         in_specs=placed,
         out_specs=(P(("grp", "row"), None, None), P(("grp", "row"), None)),

time: 63 us -> 42.8 us (0.68)
  Pallas kernels: 0 us -> 30.1 us
  waiting for transfers between devices: 28.8 us -> 0 us
  starting transfers between devices: 12.7 us -> 0 us
  matrix products: 8.16 us -> 0 us
  other arithmetic: 4.18 us -> 0.78 us
  local copies, waits for them, and re-layouts: 7.32 us -> 10.7 us
    pallas_call x0 -> x1, Pallas kernels: none -> 30.1 us  [fused(): pl.pallas_call(functools.partial(fused_kernel, devices), out_shape=(jax.S...]
    all_to_all x3 -> x0, waiting for transfers between devices: 28.8 us -> none  [the longest x1 14.1 us: per_device(): got = lax.all_to_all(sent, 'row', split_axis=0, concat_axis=0, tiled=True)]
    all_to_all x3 -> x0, starting transfers between devices: 12.7 us -> none  [the longest x1 7.3 us: per_device(): got = lax.all_to_all(sent, 'row', split_axis=0, concat_axis=0, tiled=True)]
    unnamed x29 -> x21, local copies, waits for them, and re-layouts: 1.22 us -> 9.83 us
    dot_general x20 -> x0, matrix products: 6.92 us -> none  [the longest x1 1.24 us: per_device(): jnp.einsum('ijc,cd->ijd', attended_gated, w_att_out, preferred_element_ty...]
    dynamic_update_slice x4 -> x0, local copies, waits for them, and re-layouts: 2.5 us -> none  [per_device(): attended = lax.map(attend_row, (queries, keys_in, values_in))]
    reduce_sum x8 -> x0, other arithmetic: 2.07 us -> none  [the longest x5 1.15 us: layer_norm(): spread = jnp.mean(centred * centred, axis=along_axis, keepdims=True)]
    sub x4 -> x0, matrix products: 1.24 us -> none  [row_attention(): weights = jax.nn.softmax(scores, axis=-1).astype(jnp.bfloat16)]
  transfers between devices with their start and end apart: 3 -> 0, of which waited for: 3 -> 0; matrix products, arithmetic and copies ran while one was open for 3% -> 0% of each run, Pallas kernels for 0% -> 0%
where the time goes in v2:
time: 42.8 us; the launch traced here: 42.3 us
  Pallas kernels  30.1 us (70%)
  local copies, waits for them, and re-layouts  10.7 us (25%)
  other arithmetic  0.78 us (2%)
  between operations  0.68 us (2%)
    pallas_call x1, Pallas kernels, fused(): pl.pallas_call(functools.partial(fused_kernel, devices), out_shape=(jax.S...  30.1 us
    unnamed x21, local copies, waits for them, and re-layouts  9.83 us

profile of v2, /device:TPU:0, one launch (start us, length us, event | category | flops | bytes accessed | tf_op | source)
XLA Modules:
  0.0 42.3 jit_solution(15232026686965858471)
XLA Ops:
  0.6 0.1 pad.2.clone
  0.7 0.8 %maximum_maximum_fusion.w_small = bf16[32,128]{1,0:T(8,128)(2,1)S(1)} fusion(bf16[4,128]{1,0:T(4,128)(2,1)} %bitcast.23, bf16[16,128]{1,0:T(8,128)(2,1)} %bitcast.22, bf16[32]{0:T(256)(128)(2,1)S(1)} %pad.2.clone), kind=kLoop, calls=%fused_computation | loop fusion | flops 24576 | bytes 13376 | tf_op jit(solution)/shard_map/concatenate | solution.py:370
  1.5 0.8 %copy.19 = bf16[32,4,128]{2,0,1:T(8,128)(2,1)S(1)} copy(bf16[32,4,128]{2,1,0:T(4,128)(2,1)} %bitcast.21) | data formatting | bytes 65536 | tf_op jit(solution)/shard_map/reshape | solution.py:369
  2.3 1.0 %copy.17 = bf16[128,512]{0,1:T(8,128)(2,1)S(1)} copy(bf16[128,512]{1,0:T(8,128)(2,1)} %param.17) | data formatting | bytes 262144 | tf_op args[4]
  3.3 0.0 copy-start
  3.4 1.3 %copy-done = bf16[384,1536]{1,0:T(8,128)(2,1)S(1)} copy-done((bf16[384,1536]{1,0:T(8,128)(2,1)S(1)}, bf16[384,1536]{1,0:T(8,128)(2,1)}, u32[]{:S(2)}) %copy-start) | copy-done | bytes 1179672
  4.6 0.0 copy-start.1
  4.6 1.0 %copy-done.1 = bf16[384,384]{1,0:T(8,128)(2,1)S(1)} copy-done((bf16[384,384]{1,0:T(8,128)(2,1)S(1)}, bf16[384,384]{1,0:T(8,128)(2,1)}, u32[]{:S(2)}) %copy-start.1) | copy-done | bytes 294936
  5.6 0.0 copy-start.2
  5.6 0.9 %copy-done.2 = bf16[4,128,128]{2,1,0:T(8,128)(2,1)S(1)} copy-done((bf16[4,128,128]{2,1,0:T(8,128)(2,1)S(1)}, bf16[4,128,128]{2,1,0:T(8,128)(2,1)}, u32[]{:S(2)}) %copy-start.2) | copy-done | bytes 131096
  6.5 0.0 copy-start.3
  6.5 0.9 %copy-done.3 = bf16[128,512]{1,0:T(8,128)(2,1)S(1)} copy-done((bf16[128,512]{1,0:T(8,128)(2,1)S(1)}, bf16[128,512]{1,0:T(8,128)(2,1)}, u32[]{:S(2)}) %copy-start.3) | copy-done | bytes 131096
  7.4 0.0 copy-start.4
  7.4 0.8 %copy-done.4 = bf16[128,128]{1,0:T(8,128)(2,1)S(1)} copy-done((bf16[128,128]{1,0:T(8,128)(2,1)S(1)}, bf16[128,128]{1,0:T(8,128)(2,1)}, u32[]{:S(2)}) %copy-start.4) | copy-done | bytes 32792
  8.1 0.0 copy-start.5
  8.1 0.8 %copy-done.5 = bf16[128,128]{1,0:T(8,128)(2,1)S(1)} copy-done((bf16[128,128]{1,0:T(8,128)(2,1)S(1)}, bf16[128,128]{1,0:T(8,128)(2,1)}, u32[]{:S(2)}) %copy-start.5) | copy-done | bytes 32792
  8.9 0.0 copy-start.6
  8.9 0.7 %copy-done.6 = bf16[4,384]{1,0:T(4,128)(2,1)S(1)} copy-done((bf16[4,384]{1,0:T(4,128)(2,1)S(1)}, bf16[4,384]{1,0:T(4,128)(2,1)}, u32[]{:S(2)}) %copy-start.6) | copy-done | bytes 3096
  9.6 0.0 copy-start.7
  9.6 0.7 %copy-done.7 = bf16[4,384]{1,0:T(4,128)(2,1)S(1)} copy-done((bf16[4,384]{1,0:T(4,128)(2,1)S(1)}, bf16[4,384]{1,0:T(4,128)(2,1)}, u32[]{:S(2)}) %copy-start.7) | copy-done | bytes 3096
  10.3 0.7 %copy-done.8 = s32[128]{0:T(128)S(1)} copy-done((s32[128]{0:T(128)S(1)}, s32[128]{0:T(128)}, u32[]{:S(2)}) %copy-start.8) | copy-done | bytes 536
  10.9 30.1 %shard_map.140 = (bf16[512,128]{1,0:T(8,128)(2,1)S(1)}, bf16[4,384]{1,0:T(4,128)(2,1)S(1)}) custom-call(s32[128]{0:T(128)S(1)} %copy-done.8, s32[1,128]{1,0:T(1,128)S(1)} %bitcast.19, bf16[512,128]{1,0:T(8,128)(2,1)S(1)} %bitcast.17, bf16[4,384]{1,0:T(4,128)(2,1)S(1)} %copy-done.6, bf16[4,384]{1,0:T(4,128)(2,1)S(1)} %copy-done.7, ...), custom_call_target="tpu_custom_call" | custom-call | tf_op jit(solution)/shard_map/pallas_call | solution.py:372
  41.1 0.7 %copy.22 = bf16[4,128,128]{2,1,0:T(8,128)(2,1)} copy(bf16[4,128,128]{2,1,0:T(8,128)(2,1)S(1)} %bitcast.18) | data formatting | bytes 262144
  41.7 0.6 %copy.23 = bf16[4,384]{1,0:T(4,128)(2,1)} copy(bf16[4,384]{1,0:T(4,128)(2,1)S(1)} %get-tuple-element.9) | data formatting | bytes 6144
  (3 shorter events, 0.1 us)
Async XLA Ops:
  3.3 1.3 %copy-start = (bf16[384,1536]{1,0:T(8,128)(2,1)S(1)}, bf16[384,1536]{1,0:T(8,128)(2,1)}, u32[]{:S(2)}) copy-start(bf16[384,1536]{1,0:T(8,128)(2,1)} %w_tok_in.1) | copy-start | bytes 3538948
  4.6 1.0 %copy-start.1 = (bf16[384,384]{1,0:T(8,128)(2,1)S(1)}, bf16[384,384]{1,0:T(8,128)(2,1)}, u32[]{:S(2)}) copy-start(bf16[384,384]{1,0:T(8,128)(2,1)} %w_tok_out.1) | copy-start | bytes 884740
  5.6 0.9 %copy-start.2 = (bf16[4,128,128]{2,1,0:T(8,128)(2,1)S(1)}, bf16[4,128,128]{2,1,0:T(8,128)(2,1)}, u32[]{:S(2)}) copy-start(bf16[4,128,128]{2,1,0:T(8,128)(2,1)} %param.13) | copy-start | bytes 393220
  6.5 0.9 %copy-start.3 = (bf16[128,512]{1,0:T(8,128)(2,1)S(1)}, bf16[128,512]{1,0:T(8,128)(2,1)}, u32[]{:S(2)}) copy-start(bf16[128,512]{1,0:T(8,128)(2,1)} %w_att_in.1) | copy-start | bytes 393220
  7.4 0.8 %copy-start.4 = (bf16[128,128]{1,0:T(8,128)(2,1)S(1)}, bf16[128,128]{1,0:T(8,128)(2,1)}, u32[]{:S(2)}) copy-start(bf16[128,128]{1,0:T(8,128)(2,1)} %w_mul_gate.1) | copy-start | bytes 98308
  8.1 0.8 %copy-start.5 = (bf16[128,128]{1,0:T(8,128)(2,1)S(1)}, bf16[128,128]{1,0:T(8,128)(2,1)}, u32[]{:S(2)}) copy-start(bf16[128,128]{1,0:T(8,128)(2,1)} %w_att_out.1) | copy-start | bytes 98308
  8.9 0.7 %copy-start.6 = (bf16[4,384]{1,0:T(4,128)(2,1)S(1)}, bf16[4,384]{1,0:T(4,128)(2,1)}, u32[]{:S(2)}) copy-start(bf16[4,384]{1,0:T(4,128)(2,1)} %single_ref.1) | copy-start | bytes 9220
  9.6 0.7 %copy-start.7 = (bf16[4,384]{1,0:T(4,128)(2,1)S(1)}, bf16[4,384]{1,0:T(4,128)(2,1)}, u32[]{:S(2)}) copy-start(bf16[4,384]{1,0:T(4,128)(2,1)} %noise_ref.1) | copy-start | bytes 9220
  10.3 0.7 %copy-start.8 = (s32[128]{0:T(128)S(1)}, s32[128]{0:T(128)}, u32[]{:S(2)}) copy-start(s32[128]{0:T(128)} %mask_scalar.1) | copy-start | bytes 1540

commit v3 on v2

--- a/solution.py
+++ b/solution.py
@@ -165,19 +165,18 @@
 
 def fused_kernel(
     devices,
-    mask_scalar,
-    mask_lane,
-    pair_ref,
-    single_ref,
-    noise_ref,
-    w_sides,
-    w_mul_gate,
-    w_mul_out,
-    w_att_in,
-    w_small,
-    w_att_out,
-    w_tok_in,
-    w_tok_out,
+    *refs,
+):
+    operands, (pair_out, token_out), refs = refs[:13], refs[13:15], refs[15:]
+    held, local_sem, refs = refs[:13], refs[13], refs[14:]
+    kernel_body(devices, operands, held, local_sem, pair_out, token_out, *refs)
+
+
+def kernel_body(
+    devices,
+    operands,
+    held,
+    local_sem,
     pair_out,
     token_out,
     send_sides,
@@ -195,12 +194,36 @@
     wide_all,
     wide_kv,
     wide_keys,
+    wide_w,
+    w_sides,
+    wide_out,
     send_sem,
     recv_sem,
 ):
     f32 = jnp.float32
     bf16 = jnp.bfloat16
     me = lax.axis_index("row")
+    (
+        pair_ref,
+        single_ref,
+        noise_ref,
+        mask_lane,
+        w_mul_in,
+        w_mul_gate,
+        w_mul_out,
+        w_att_in,
+        w_att_bias,
+        w_att_out,
+        w_tok_in,
+        w_pair_bias,
+        w_tok_out,
+    ) = held
+    loads = [
+        pltpu.make_async_copy(source, target, local_sem.at[index])
+        for index, (source, target) in enumerate(zip(operands, held))
+    ]
+    for index in (0, 4, 3, 1, 2, 10, 5, 6, 7, 8, 9, 11, 12):
+        loads[index].start()
 
     barrier = pltpu.get_barrier_semaphore()
 
@@ -232,14 +255,24 @@
         whole = landing.at[pl.ds(0, devices - 1)]
         pltpu.make_async_copy(whole, whole, sem).wait()
 
+    loads[4].wait()
+    wide_w[...] = w_mul_in[...].astype(f32).T
+    for kind in range(4):
+        for c in range(4):
+            w_sides[pl.ds((kind % 2) * 256 + (kind // 2) * 4 + c, devices, stride=8), :] = wide_w[
+                pl.ds(kind * 128 + c, devices, stride=4), :
+            ]
+    loads[0].wait()
+    loads[3].wait()
     pair = pair_ref[...].astype(f32)
     normed = lane_norm(pair)
-    mixed = dot_nt(w_sides[...], normed)
+    mixed = dot_nt(w_sides[...].astype(bf16), normed)
     mask = mask_lane[...].astype(f32)
+    place = lax.broadcasted_iota(jnp.int32, mask.shape, 1)
     half = w_sides.shape[0] // 2
     blocks = []
     for i in range(4):
-        mask_row = mask_scalar[me * 4 + i].astype(f32)
+        mask_row = jnp.sum(jnp.where(place == me * 4 + i, mask, 0.0), axis=1, keepdims=True)
         cols = slice(i * 128, (i + 1) * 128)
         side = jax.nn.sigmoid(mixed[:half, cols]) * mixed[half:, cols] * (mask * mask_row)
         blocks.append(side.reshape(devices, 8, 128))
@@ -248,6 +281,8 @@
     pl.semaphore_wait(barrier, devices - 1)
     send_all(0, lambda other: send_sides.at[other], recv_sides)
 
+    for index in (1, 2, 10):
+        loads[index].wait()
     activity = single_ref[...].astype(f32) + noise_ref[...].astype(f32)
     activity = jnp.concatenate([activity, jnp.zeros_like(activity)], axis=0)
     tok = dot_nn(lane_norm(activity), w_tok_in[...])
@@ -257,7 +292,16 @@
         wide_kv[pl.ds(m, 4, stride=8), :] = tok[:4, width + m * 128 : width + (m + 1) * 128]
     send_kv[...] = wide_kv[...].astype(bf16)
     recv_kv[me] = send_kv[...]
+    for index in (5, 6, 7, 8, 9, 11, 12):
+        loads[index].wait()
     gating = jax.nn.sigmoid(dot_nn(normed, w_mul_gate[...]))
+    wide_out[...] = w_mul_out[...].astype(f32)
+    w_back = jnp.concatenate(
+        [wide_out[pl.ds(c, devices, stride=4), :] for c in range(4)], axis=0
+    ).astype(bf16)
+    w_att_bias_t = jnp.concatenate(
+        [w_att_bias[...].astype(f32), jnp.zeros((12, 128), f32)], axis=0
+    ).astype(bf16)
 
     wait_all(recv_sem.at[0], recv_sides)
     wide_sides[...] = recv_sides[...].astype(f32).reshape(wide_sides.shape)
@@ -277,11 +321,11 @@
             [wide_back[pl.ds(i * 4 + c, devices, stride=16), :] for c in range(4)], axis=0
         )
         crossed_norm.append(layer_norm(crossed, 0).T.astype(bf16))
-    update = dot_nn(jnp.concatenate(crossed_norm, axis=0), w_mul_out[...])
+    update = dot_nn(jnp.concatenate(crossed_norm, axis=0), w_back)
     pair_one = (pair + gating * update).astype(bf16).astype(f32)
 
     normed_one = lane_norm(pair_one)
-    bias = dot_nt(w_small[16:32], normed_one)
+    bias = dot_nt(w_att_bias_t, normed_one)
     for i in range(4):
         wide_bias[i * 4 : (i + 1) * 4, :] = bias[:4, i * 128 : (i + 1) * 128]
     send_bias[...] = wide_bias[...].astype(bf16)
@@ -315,7 +359,7 @@
     final = (pair_one + dot_nn(jnp.concatenate(gated, axis=0), w_att_out[...])).astype(bf16)
     pair_out[...] = final
 
-    pair_bias = dot_nt(w_small[0:16], lane_norm(final.astype(f32))).astype(bf16).astype(f32)
+    pair_bias = dot_nt(w_pair_bias[...], lane_norm(final.astype(f32))).astype(bf16).astype(f32)
     pair_bias = jnp.concatenate([pair_bias[:, i * 128 : (i + 1) * 128] for i in range(4)], axis=0)
     lane = lax.broadcasted_iota(jnp.int32, (16, width), 1)
     head = lax.broadcasted_iota(jnp.int32, (16, width), 0)
@@ -363,11 +407,21 @@
     bf16 = jnp.bfloat16
     f32 = jnp.float32
     devices = lax.axis_size("row")
-    w_sides = (
-        w_mul_in.T.reshape(2, 2, devices, 4, 128).transpose(1, 2, 0, 3, 4).reshape(512, 128)
-    )
-    w_back = w_mul_out.reshape(devices, 4, 128).transpose(1, 0, 2).reshape(128, 128)
-    w_small = jnp.concatenate([w_pair_bias.T, w_att_bias.T, jnp.zeros((12, 128), bf16)], axis=0)
+    operands = (
+        pair_map.reshape(512, 128),
+        single,
+        noise_term,
+        token_mask.reshape(1, -1),
+        w_mul_in,
+        w_mul_gate,
+        w_mul_out,
+        w_att_in,
+        w_att_bias.T,
+        w_att_out,
+        w_tok_in,
+        w_pair_bias.T,
+        w_tok_out,
+    )
     vmem = pl.BlockSpec(memory_space=pltpu.VMEM)
     pair_out, token_out = pl.pallas_call(
         functools.partial(fused_kernel, devices),
@@ -375,9 +429,11 @@
             jax.ShapeDtypeStruct((512, 128), bf16),
             jax.ShapeDtypeStruct(single.shape, bf16),
         ),
-        in_specs=[pl.BlockSpec(memory_space=pltpu.SMEM)] + [vmem] * 12,
+        in_specs=[pl.BlockSpec(memory_space=pl.ANY)] * 13,
         out_specs=(vmem, vmem),
-        scratch_shapes=[
+        scratch_shapes=[pltpu.VMEM(held.shape, held.dtype) for held in operands]
+        + [
+            pltpu.SemaphoreType.DMA((13,)),
             pltpu.VMEM((devices, 32, 128), bf16),
             pltpu.VMEM((devices, 32, 128), bf16),
             pltpu.VMEM((devices, 16, 128), bf16),
@@ -393,27 +449,16 @@
             pltpu.VMEM((devices * 16, 128), f32),
             pltpu.VMEM((32, 128), f32),
             pltpu.VMEM((devices * 32, 128), f32),
+            pltpu.VMEM((512, 128), f32),
+            pltpu.VMEM((512, 128), f32),
+            pltpu.VMEM((128, 128), f32),
             pltpu.SemaphoreType.DMA((4,)),
             pltpu.SemaphoreType.DMA((4,)),
         ],
         compiler_params=pltpu.CompilerParams(
-            collective_id=0, has_side_effects=True, vmem_limit_bytes=40 * 1024 * 1024
+            collective_id=0, has_side_effects=True, vmem_limit_bytes=56 * 1024 * 1024
         ),
-    )(
-        token_mask,
-        token_mask.reshape(1, -1),
-        pair_map.reshape(512, 128),
-        single,
-        noise_term,
-        w_sides,
-        w_mul_gate,
-        w_back,
-        w_att_in,
-        w_small,
-        w_att_out,
-        w_tok_in,
-        w_tok_out,
-    )
+    )(*operands)
     return pair_out.reshape(pair_map.shape), token_out
 
 

time: 42.8 us -> 34 us (0.79)
  local copies, waits for them, and re-layouts: 10.7 us -> 2.83 us
  other arithmetic: 0.78 us -> 0 us
    unnamed x21 -> x2, local copies, waits for them, and re-layouts: 9.83 us -> 2.83 us
    concatenate x1 -> x0, other arithmetic: 0.78 us -> none  [fused(): jnp.concatenate([w_pair_bias.T, w_att_bias.T, jnp.zeros((12, 128), bf16)]...]
    reshape x1 -> x0, local copies, waits for them, and re-layouts: 0.76 us -> none  [fused(): w_mul_out.reshape(devices, 4, 128).transpose(1, 0, 2).reshape(128, 128)]
where the time goes in v3:
time: 34 us; the launch traced here: 33.8 us
  Pallas kernels  30.4 us (89%)
  local copies, waits for them, and re-layouts  2.83 us (8%)
  between operations  0.64 us (2%)
    pallas_call x1, Pallas kernels, fused(): pl.pallas_call(functools.partial(fused_kernel, devices), out_shape=(jax.S...  30.4 us
    unnamed x2, local copies, waits for them, and re-layouts  2.83 us

profile of v3, /device:TPU:0, one launch (start us, length us, event | category | flops | bytes accessed | tf_op | source)
XLA Modules:
  0.0 33.8 jit_solution(11038646766438925396)
XLA Ops:
  0.6 30.4 %shard_map.140 = (bf16[512,128]{1,0:T(8,128)(2,1)}, bf16[4,384]{1,0:T(4,128)(2,1)}) custom-call(bf16[512,128]{1,0:T(8,128)(2,1)} %bitcast.5, bf16[4,384]{1,0:T(4,128)(2,1)} %refs_1_.1, bf16[4,384]{1,0:T(4,128)(2,1)} %refs_2_.1, s32[1,128]{1,0:T(1,128)} %bitcast.9, bf16[128,512]{1,0:T(8,128)(2,1)} %refs_4_.1, bf16[128,128]{1,0:T(8,128)(2,1)} %refs_5_.1, ...), custom_call_target="tpu_custom_call" | custom-call | tf_op jit(solution)/shard_map/pallas_call | solution.py:426
  31.0 1.6 %copy.17 = bf16[4,128,128]{2,1,0:T(8,128)(2,1)} copy(bf16[4,128,128]{2,1,0:T(8,128)(2,1)} %bitcast.6) | data formatting | bytes 262144
  32.6 1.3 %copy.18 = bf16[4,384]{1,0:T(4,128)(2,1)} copy(bf16[4,384]{1,0:T(4,128)(2,1)} %get-tuple-element.9) | data formatting | bytes 6144

commit v4 on v3

--- a/solution.py
+++ b/solution.py
@@ -234,7 +234,7 @@
         )
         return carry
 
-    lax.fori_loop(1, devices, greet, 0)
+    lax.fori_loop(1, devices, greet, 0, unroll=True)
 
     def send_all(slot, source, landing):
         def one(step, carry):
@@ -249,11 +249,48 @@
             ).start()
             return carry
 
-        lax.fori_loop(1, devices, one, 0)
+        lax.fori_loop(1, devices, one, 0, unroll=True)
 
     def wait_all(sem, landing):
         whole = landing.at[pl.ds(0, devices - 1)]
         pltpu.make_async_copy(whole, whole, sem).wait()
+
+    depth = 4
+    plane = devices // depth
+    level = lax.div(me, plane)
+    seat = lax.rem(me, plane)
+
+    def hop(slot, source, landing, target, other):
+        pltpu.make_async_remote_copy(
+            src_ref=source,
+            dst_ref=landing.at[target],
+            send_sem=send_sem.at[slot],
+            recv_sem=recv_sem.at[slot],
+            device_id={"row": other},
+            device_id_type=pl.DeviceIdType.MESH,
+        ).start()
+
+    def first_hop(slot, source, landing):
+        for step in range(1, depth):
+            other = lax.rem(level + step, depth) * plane + seat
+            hop(slot, source, landing, seat * depth + level, other)
+
+    def second_hop(slot, landing):
+        wait_bytes(recv_sem.at[slot - 1], landing, depth - 1)
+        bundle = pl.ds(seat * depth, depth)
+        for step in range(1, plane):
+            other = level * plane + lax.rem(seat + step, plane)
+            hop(slot, landing.at[bundle], landing, bundle, other)
+
+    def wait_bytes(sem, landing, count):
+        some = landing.at[pl.ds(0, count)]
+        pltpu.make_async_copy(some, some, sem).wait()
+
+    def in_order(landing, wide):
+        size = landing.shape[1]
+        for position in range(devices):
+            start = ((position % depth) * plane + position // depth) * size
+            wide[start : start + size, :] = landing[position].astype(f32)
 
     loads[4].wait()
     wide_w[...] = w_mul_in[...].astype(f32).T
@@ -291,7 +328,8 @@
     for m in range(6):
         wide_kv[pl.ds(m, 4, stride=8), :] = tok[:4, width + m * 128 : width + (m + 1) * 128]
     send_kv[...] = wide_kv[...].astype(bf16)
-    recv_kv[me] = send_kv[...]
+    recv_kv[seat * depth + level] = send_kv[...]
+    first_hop(2, send_kv, recv_kv)
     for index in (5, 6, 7, 8, 9, 11, 12):
         loads[index].wait()
     gating = jax.nn.sigmoid(dot_nn(normed, w_mul_gate[...]))
@@ -312,7 +350,6 @@
     send_prod[...] = wide_prod[...].astype(bf16).reshape(send_prod.shape)
     recv_prod[me] = send_prod[me]
     send_all(1, lambda other: send_prod.at[other], recv_prod)
-    send_all(3, lambda other: send_kv, recv_kv)
     wait_all(recv_sem.at[1], recv_prod)
     wide_back[...] = recv_prod[...].astype(f32).reshape(wide_back.shape)
     crossed_norm = []
@@ -330,7 +367,8 @@
         wide_bias[i * 4 : (i + 1) * 4, :] = bias[:4, i * 128 : (i + 1) * 128]
     send_bias[...] = wide_bias[...].astype(bf16)
     recv_bias[me] = send_bias[...]
-    send_all(2, lambda other: send_bias, recv_bias)
+    send_all(4, lambda other: send_bias, recv_bias)
+    second_hop(3, recv_kv)
     projected = dot_nn(normed_one, w_att_in[...])
     shift = jnp.where(mask > 0, 0.0, -1000000000.0).astype(f32)
     head_of = lax.broadcasted_iota(jnp.int32, (128, 128), 1) // 32
@@ -341,7 +379,7 @@
         query = jnp.concatenate([jnp.where(head_of == h, query, 0.0) for h in range(4)], axis=0)
         raw.append(dot_nt(query.astype(bf16), projected[rows, 128:256].astype(bf16)))
 
-    wait_all(recv_sem.at[2], recv_bias)
+    wait_all(recv_sem.at[4], recv_bias)
     wide_all[...] = recv_bias[...].astype(f32).reshape(wide_all.shape)
     bias_all = jnp.concatenate(
         [wide_all[pl.ds(h, 128, stride=4), :] for h in range(4)], axis=0
@@ -365,8 +403,8 @@
     head = lax.broadcasted_iota(jnp.int32, (16, width), 0)
     own = (lane >= head * 24) & (lane < head * 24 + 24)
     query = jnp.concatenate([jnp.where(own, tok[i : i + 1, :width], 0.0) for i in range(4)], axis=0)
-    wait_all(recv_sem.at[3], recv_kv)
-    wide_keys[...] = recv_kv[...].astype(f32).reshape(wide_keys.shape)
+    wait_bytes(recv_sem.at[3], recv_kv, devices - depth)
+    in_order(recv_kv, wide_keys)
     chunks = [wide_keys[pl.ds(m, 128, stride=8), :].astype(bf16) for m in range(6)]
     keys = jnp.concatenate(chunks[:3], axis=1)
     values = jnp.concatenate(chunks[3:], axis=1)
@@ -385,8 +423,9 @@
 
     wait_all(send_sem.at[0], recv_sides)
     wait_all(send_sem.at[1], recv_prod)
-    wait_all(send_sem.at[2], recv_bias)
-    wait_all(send_sem.at[3], recv_kv)
+    wait_all(send_sem.at[4], recv_bias)
+    wait_bytes(send_sem.at[2], recv_kv, depth - 1)
+    wait_bytes(send_sem.at[3], recv_kv, devices - depth)
 
 
 def fused(
@@ -452,8 +491,8 @@
             pltpu.VMEM((512, 128), f32),
             pltpu.VMEM((512, 128), f32),
             pltpu.VMEM((128, 128), f32),
-            pltpu.SemaphoreType.DMA((4,)),
-            pltpu.SemaphoreType.DMA((4,)),
+            pltpu.SemaphoreType.DMA((6,)),
+            pltpu.SemaphoreType.DMA((6,)),
         ],
         compiler_params=pltpu.CompilerParams(
             collective_id=0, has_side_effects=True, vmem_limit_bytes=56 * 1024 * 1024

time: 34 us -> 32.4 us (0.953)
  Pallas kernels: 30.4 us -> 28.7 us
    pallas_call x1, Pallas kernels: 30.4 us -> 28.7 us  [fused(): pl.pallas_call(functools.partial(fused_kernel, devices), out_shape=(jax.S...]
where the time goes in v4:
time: 32.4 us; the launch traced here: 32.2 us
  Pallas kernels  28.7 us (89%)
  local copies, waits for them, and re-layouts  2.83 us (9%)
  between operations  0.64 us (2%)
    pallas_call x1, Pallas kernels, fused(): pl.pallas_call(functools.partial(fused_kernel, devices), out_shape=(jax.S...  28.7 us
    unnamed x2, local copies, waits for them, and re-layouts  2.83 us

profile of v4, /device:TPU:0, one launch (start us, length us, event | category | flops | bytes accessed | tf_op | source)
XLA Modules:
  0.0 32.2 jit_solution(2960813091055302403)
XLA Ops:
  0.6 28.7 %shard_map.140 = (bf16[512,128]{1,0:T(8,128)(2,1)}, bf16[4,384]{1,0:T(4,128)(2,1)}) custom-call(bf16[512,128]{1,0:T(8,128)(2,1)} %bitcast.5, bf16[4,384]{1,0:T(4,128)(2,1)} %refs_1_.1, bf16[4,384]{1,0:T(4,128)(2,1)} %refs_2_.1, s32[1,128]{1,0:T(1,128)} %bitcast.9, bf16[128,512]{1,0:T(8,128)(2,1)} %refs_4_.1, bf16[128,128]{1,0:T(8,128)(2,1)} %refs_5_.1, ...), custom_call_target="tpu_custom_call" | custom-call | tf_op jit(solution)/shard_map/pallas_call | solution.py:465
  29.4 1.6 %copy.17 = bf16[4,128,128]{2,1,0:T(8,128)(2,1)} copy(bf16[4,128,128]{2,1,0:T(8,128)(2,1)} %bitcast.6) | data formatting | bytes 262144
  30.9 1.3 %copy.18 = bf16[4,384]{1,0:T(4,128)(2,1)} copy(bf16[4,384]{1,0:T(4,128)(2,1)} %get-tuple-element.9) | data formatting | bytes 6144
